TPU v7x, 256 devices: a whole 4x4x8 slice. The times are simulated.
256 devices in a mesh: tile: 16 (over z, core), lev: 4 (over x), tag: 4 (over y).
Axes of the slice: x: 4, y: 4, z: 8, core: 2. Of those that a mesh axis runs over, the one named last changes fastest.
Arguments:
- parent_field: float32 [8, 32, 256, 1024], P('tag', 'lev', 'tile'), may hold values from -6 to 6
- nest_field: float32 [8, 32, 256, 1024], P('tag', 'lev', 'tile'), may hold values from -6 to 6
- parent_mixing: float32 [32, 256, 1024], P('lev', 'tile'), may hold values from 0.05 to 5
- parent_eastward: float32 [256, 1024], P('tile'), may hold values from 0.02 to 0.12
- parent_northward: float32 [256, 1024], P('tile'), may hold values from 0.02 to 0.12
- nest_eastward: float32 [256, 1024], P('tile'), may hold values from 0.02 to 0.12
- nest_northward: float32 [256, 1024], P('tile'), may hold values from 0.02 to 0.12
- strip_tile: int32 [16, 256], replicated, may hold values from 0 to 15, as said below
- strip_block: int32 [16, 256], replicated, may hold values from 0 to 127
- strip_target: int32 [16, 256], replicated, may hold values from 0 to 127
- strip_count: int32 [16], replicated, may hold values from 1 to 256, as said below
Outputs:
- parent_adjoint: float32 [8, 32, 256, 1024], P('tag', 'lev', 'tile')
- nest_adjoint: float32 [8, 32, 256, 1024], P('tag', 'lev', 'tile')
- bulk_adjoint: float32 [32, 256, 1024], P('lev', 'tile', 'tag')
Inputs may be any that keep to these rules, and one draw needn't show every extreme that they name: `strip_tile`: among the first strip_count[j] entries of row j, every parent tile appears at most 16 times; in the row whose count is 256 every parent tile appears exactly 16 times. `strip_count`: exactly one nest tile lists 256 strips; every other lists at most 128.
All inputs are finite; a program needn't handle non-finite values.
Results may differ from a plain program's by a relative error of at most 0.0003.
Values sent between devices are 32-bit elements; how exact they have to be, the bound alone decides.
A program may use at most 64 MiB of HBM per device.

v0:
```python
import jax
import jax.numpy as jnp
from jax import lax
from jax.sharding import PartitionSpec as P

CAP = 16
NSUB = 3
HIGHEST = lax.Precision.HIGHEST


def extended(cells, sides, width):
    for axis, dim in sides:
        count = lax.axis_size(axis)
        ends = count - 1
        head = lax.slice_in_dim(cells, 0, width, axis=dim)
        tail = lax.slice_in_dim(cells, cells.shape[dim] - width, cells.shape[dim], axis=dim)
        cells = jnp.concatenate(
            [
                lax.ppermute(tail, axis, [(i, (i + 1) % count) for i in range(ends)]),
                cells,
                lax.ppermute(head, axis, [((i + 1) % count, i) for i in range(ends)]),
            ],
            axis=dim,
        )
    return cells


def tridiagonal(source, mixing):
    level_count = mixing.shape[0]
    mixing_up = jnp.concatenate([mixing[1:], jnp.zeros_like(mixing[:1])], axis=0)
    diagonal = 1.0 + mixing + mixing_up
    ratio_now = jnp.zeros_like(mixing[0])
    carry_now = jnp.zeros_like(source[:, 0])
    ratios = []
    carries = []
    for lev_index in range(level_count):
        pivot_now = diagonal[lev_index] + mixing[lev_index] * ratio_now
        ratio_now = -mixing_up[lev_index] / pivot_now
        carry_now = (source[:, lev_index] + mixing[lev_index] * carry_now) / pivot_now
        ratios.append(ratio_now)
        carries.append(carry_now)
    value_now = carries[level_count - 1]
    results = [value_now]
    for lev_index in range(level_count - 2, -1, -1):
        value_now = carries[lev_index] - ratios[lev_index] * value_now
        results.append(value_now)
    return jnp.stack(results[::-1], axis=1)


def relax(padded, eastward):
    center = padded[:-1, 1:-1]
    row_above = padded[:-1, :-2]
    row_below = padded[:-1, 2:]
    north_here = padded[-1, 1:-1]
    north_above = padded[-1, :-2]
    zero_column = jnp.zeros_like(center[:, :, :1])
    east_cell = jnp.concatenate([center[:, :, 1:], zero_column], axis=2)
    west_cell = jnp.concatenate([zero_column, center[:, :, :-1]], axis=2)
    west_rate = jnp.concatenate([jnp.zeros_like(eastward[:, :1]), eastward[:, :-1]], axis=1)
    return (
        center
        + north_here * (row_below - center)
        + north_above * (row_above - center)
        + eastward * (east_cell - center)
        + west_rate * (west_cell - center)
    )


def rims(stacked):
    return extended(stacked, (("tile", 1),), 1)


def advance(start, solved, parent_eastward, parent_northward, nest_eastward, nest_northward):
    tag_count, level_count, row_count, col_count = start.shape
    line_count = tag_count * level_count
    nest_now = start.reshape(line_count, row_count, col_count)
    parent_now = solved.reshape(line_count, row_count, col_count)
    for sub_step in range(NSUB):
        nest_stack = jnp.concatenate([nest_now, nest_northward[None]], axis=0)
        if sub_step == 0:
            parent_stack = jnp.concatenate([parent_now, parent_northward[None]], axis=0)
            padded = rims(jnp.concatenate([parent_stack, nest_stack], axis=0))
            parent_now = relax(padded[: line_count + 1], parent_eastward)
            nest_now = relax(padded[line_count + 1 :], nest_eastward)
        else:
            nest_now = relax(rims(nest_stack), nest_eastward)
    full_shape = (tag_count, level_count, row_count, col_count)
    return (parent_now.reshape(full_shape), nest_now.reshape(full_shape))


def deliver(parent_field, strip_tile, strip_block, strip_target, strip_count):
    tag_count, level_count, row_count, col_count = parent_field.shape
    line_count = tag_count * level_count
    block_count = row_count * col_count // 128
    tile_count, slot_total = strip_tile.shape
    own_index = lax.axis_index("tile")
    positions = jnp.arange(slot_total, dtype=jnp.int32)
    is_live = positions[None, :] < strip_count[:, None]
    from_here = jnp.logical_and(is_live, strip_tile == own_index).astype(jnp.int32)
    slot_rank = jnp.cumsum(from_here, axis=1) - 1
    slot_index = jnp.arange(CAP, dtype=jnp.int32)
    select = from_here[:, None, :] * (slot_rank[:, None, :] == slot_index[None, :, None]).astype(
        jnp.int32
    )
    source_block = jnp.sum(select * strip_block[:, None, :], axis=2).reshape(-1)
    filled = jnp.sum(select, axis=2).reshape(-1).astype(jnp.float32)
    blocks = parent_field.reshape(line_count, block_count, 128)
    packed = jnp.take(blocks, source_block, axis=1) * filled[None, :, None]
    received = lax.all_to_all(packed, "tile", split_axis=1, concat_axis=1, tiled=True)
    own_tile = lax.dynamic_index_in_dim(strip_tile, own_index, 0, keepdims=False)
    own_target = lax.dynamic_index_in_dim(strip_target, own_index, 0, keepdims=False)
    own_count = lax.dynamic_index_in_dim(strip_count, own_index, 0, keepdims=False)
    own_live = (positions < own_count).astype(jnp.int32)
    from_source = (own_tile[:, None] == jnp.arange(tile_count, dtype=jnp.int32)[None, :]).astype(
        jnp.int32
    ) * own_live[:, None]
    own_rank = jnp.sum((jnp.cumsum(from_source, axis=0) - 1) * from_source, axis=1)
    arrival = own_tile * CAP + own_rank
    pick_slot = (arrival[:, None] == jnp.arange(tile_count * CAP, dtype=jnp.int32)[None, :]).astype(
        jnp.float32
    )
    pick_slot = pick_slot * own_live[:, None].astype(jnp.float32)
    place_block = (own_target[:, None] == jnp.arange(block_count, dtype=jnp.int32)[None, :]).astype(
        jnp.float32
    )
    routing = jnp.dot(pick_slot.T, place_block, precision=HIGHEST)
    forcing = jnp.einsum("lic,ib->lbc", received, routing, precision=HIGHEST)
    return forcing.reshape(tag_count, level_count, row_count, col_count)


def shards(
    parent_field,
    nest_field,
    parent_mixing,
    parent_eastward,
    parent_northward,
    nest_eastward,
    nest_northward,
    strip_tile,
    strip_block,
    strip_target,
    strip_count,
):
    tag_count = parent_field.shape[0]
    forcing = deliver(parent_field, strip_tile, strip_block, strip_target, strip_count)
    stacked = jnp.concatenate([parent_field, parent_mixing[None]], axis=0)
    columns = lax.all_to_all(stacked, "lev", split_axis=3, concat_axis=1, tiled=True)
    column_result = tridiagonal(columns[:tag_count], columns[tag_count])
    solved = lax.all_to_all(column_result, "lev", split_axis=1, concat_axis=3, tiled=True)
    parent_adjoint, nest_adjoint = advance(
        nest_field + forcing,
        solved,
        parent_eastward,
        parent_northward,
        nest_eastward,
        nest_northward,
    )
    bulk_adjoint = lax.psum_scatter(
        jnp.sum(parent_adjoint, axis=0), "tag", scatter_dimension=2, tiled=True
    )
    return (parent_adjoint, nest_adjoint, bulk_adjoint)


def solution(mesh):
    in_specs = (
        P("tag", "lev", "tile", None),
        P("tag", "lev", "tile", None),
        P("lev", "tile", None),
        P("tile", None),
        P("tile", None),
        P("tile", None),
        P("tile", None),
        P(),
        P(),
        P(),
        P(),
    )
    out_specs = (
        P("tag", "lev", "tile", None),
        P("tag", "lev", "tile", None),
        P("lev", "tile", "tag"),
    )
    return jax.shard_map(shards, mesh=mesh, in_specs=in_specs, out_specs=out_specs, check_vma=False)
```

profile of v0, /device:TPU:2, one launch (start us, length us, event | category | flops | bytes accessed | tf_op | source)
XLA Modules:
  0.0 209.8 jit_solution(3081090923372214536)
XLA Ops:
  7.2 1.5 pad_maximum_fusion.5
  8.7 6.9 %copy.55 = f32[3,8,16,1024]{2,1,0,3:T(8,128)} copy(f32[3,8,16,1024]{3,2,1,0:T(8,128)S(1)} %pad_maximum_fusion.5) | data formatting | bytes 3145728 | tf_op jit(solution)/shard_map/concatenate | solution.py:146
  15.6 8.3 %reshape.176 = f32[4,1,98304]{2,1,0:T(1,128)} reshape(f32[1024,3,8,16]{3,2,1,0:T(8,128)} %bitcast.230) | data formatting | bytes 3145728
  23.9 5.9 %all-to-all-start = ((f32[4,1,98304]{2,1,0:T(1,128)}), f32[4,1,98304]{2,1,0:T(1,128)S(1)}, u32[]{:S(2)}, u32[]{:S(2)}) async-start(f32[4,1,98304]{2,1,0:T(1,128)} %reshape.176), calls=%async_computation | async-start | bytes 3145728 | tf_op jit(solution)/shard_map/all_to_all | solution.py:147
  32.7 1.8 copy.65
  34.7 13.4 %all-to-all-done = f32[4,1,98304]{2,1,0:T(1,128)S(1)} async-done(((f32[4,1,98304]{2,1,0:T(1,128)}), f32[4,1,98304]{2,1,0:T(1,128)S(1)}, u32[]{:S(2)}, u32[]{:S(2)}) %all-to-all-start) | async-done | bytes 1572896 | tf_op jit(solution)/shard_map/all_to_all | solution.py:147
  48.1 1.2 copy-done.1
  49.8 6.2 %reduce.4 = f32[4,98304]{1,0:T(4,128)S(1)} reduce(f32[4,1,98304]{2,1,0:T(1,128)} %copy-done.1, f32[]{:T(128)} %broadcast.2764), dimensions={1}, to_apply=%all_to_all.25.reduce_sub_computation | reduce | bytes 3145732 | tf_op jit(solution)/shard_map/all_to_all | solution.py:147
  55.9 8.9 %reshape.177 = f32[1024,3,8,16]{3,2,1,0:T(8,128)} reshape(f32[4,98304]{1,0:T(4,128)S(1)} %reduce.4) | data formatting | bytes 3145728
  64.8 7.8 %copy.69 = f32[3,8,16,4,256]{4,3,2,1,0:T(4,128)S(1)} copy(f32[3,8,16,4,256]{2,1,0,4,3:T(8,128)} %bitcast.231) | data formatting | bytes 3145728 | tf_op jit(solution)/shard_map/all_to_all | solution.py:147
  75.9 5.7 %all-to-all-start.1 = ((f32[2,32,16,256]{3,2,0,1:T(8,128)}), f32[2,32,16,256]{3,2,0,1:T(8,128)}, u32[]{:S(2)}, u32[]{:S(2)}) async-start(f32[2,32,16,256]{3,2,0,1:T(8,128)} %copy.59), calls=%async_computation.1 | async-start | bytes 2097152 | tf_op jit(solution)/shard_map/all_to_all | solution.py:149
  82.6 2.5 %multiply_bitcast_fusion = f32[16,256,128]{2,0,1:T(8,128)} fusion(f32[256,16,128]{2,1,0:T(8,128)S(1)} %gather_fusion, f32[256]{0:T(256)S(1)} %convert_element_type.43, pred[256]{0:T(512)(128)(4,1)S(1)} %compare_and_fusion), kind=kLoop, calls=%fused_computation.5 | loop fusion | flops 1048576 | bytes 4195584 | tf_op jit(solution)/shard_map/mul | solution.py:108
  85.2 8.3 %all-to-all-done.1 = f32[2,32,16,256]{3,2,0,1:T(8,128)} async-done(((f32[2,32,16,256]{3,2,0,1:T(8,128)}), f32[2,32,16,256]{3,2,0,1:T(8,128)}, u32[]{:S(2)}, u32[]{:S(2)}) %all-to-all-start.1) | async-done | bytes 1048608 | tf_op jit(solution)/shard_map/all_to_all | solution.py:149
  93.4 9.6 %all-to-all-start.2 = ((f32[16,256,128]{2,0,1:T(8,128)}), f32[16,256,128]{2,0,1:T(8,128)}, u32[]{:S(2)}, u32[]{:S(2)}) async-start(f32[16,256,128]{2,0,1:T(8,128)} %multiply_bitcast_fusion), calls=%async_computation.2 | async-start | bytes 4194304 | tf_op jit(solution)/shard_map/all_to_all | solution.py:109
  107.9 1.9 copy.61
  110.4 1.7 fusion.137
  112.1 40.2 %all-to-all-done.2 = f32[16,256,128]{2,0,1:T(8,128)} async-done(((f32[16,256,128]{2,0,1:T(8,128)}), f32[16,256,128]{2,0,1:T(8,128)}, u32[]{:S(2)}, u32[]{:S(2)}) %all-to-all-start.2) | async-done | bytes 2097184 | tf_op jit(solution)/shard_map/all_to_all | solution.py:109
  152.3 3.4 %fusion.4 = f32[16,128,128]{2,1,0:T(8,128)S(1)} fusion(f32[256,128,1]{0,1,2:T(8,128)S(1)} %convolution_bitcast_fusion, f32[16,256,128]{2,0,1:T(8,128)} %all-to-all-done.2), kind=kOutput, calls=%fused_computation.12 | convolution fusion | flops 805306368 | bytes 3276800 | tf_op jit(solution)/shard_map/lic,ib->lbc/dot_general | solution.py:127
  155.9 1.4 add.2442
  157.5 2.1 collective-permute-start.1
  159.6 1.3 collective-permute-start
  161.3 1.5 collective-permute-done
  163.6 1.7 fusion.135
  165.4 5.2 %collective-permute-start.3 = (f32[17,1,1024]{2,1,0:T(1,128)S(1)}, f32[17,1,1024]{2,1,0:T(1,128)S(1)}, u32[]{:S(2)}, u32[]{:S(2)}) collective-permute-start(f32[17,1,1024]{2,1,0:T(1,128)S(1)} %get-tuple-element.88), channel_id=1, source_target_pairs={{0,16},{16,32},{32,48},{48,64},{64,80},{80,96},{96,112},{112,128},... | collective-permute-start | bytes 208904 | tf_op jit(solution)/shard_map/ppermute | solution.py:19
  170.7 1.5 collective-permute-start.2
  172.2 1.7 fusion.35
  173.9 2.1 %reduce_sum.39 = f32[8,16,1024]{2,1,0:T(8,128)} reduce(f32[2,8,16,1024]{3,2,1,0:T(8,128)} %bitcast.265, f32[]{:T(128)} %constant.48.clone.1), dimensions={0}, to_apply=%region_7.8 | reduce | flops 131072 | bytes 1572868 | tf_op jit(solution)/shard_map/reduce_sum | solution.py:159
  178.4 3.0 %collective-permute-start.5 = (f32[17,1,1024]{2,1,0:T(1,128)S(1)}, f32[17,1,1024]{2,1,0:T(1,128)S(1)}, u32[]{:S(2)}, u32[]{:S(2)}) collective-permute-start(f32[17,1,1024]{2,1,0:T(1,128)S(1)} %get-tuple-element.86), channel_id=1, source_target_pairs={{0,16},{16,32},{32,48},{48,64},{64,80},{80,96},{96,112},{112,128},... | collective-permute-start | bytes 208904 | tf_op jit(solution)/shard_map/ppermute | solution.py:19
  181.8 1.3 collective-permute-start.4
  183.4 2.3 %collective-permute-done.4 = f32[17,1,1024]{2,1,0:T(1,128)S(1)} collective-permute-done((f32[17,1,1024]{2,1,0:T(1,128)S(1)}, f32[17,1,1024]{2,1,0:T(1,128)S(1)}, u32[]{:S(2)}, u32[]{:S(2)}) %collective-permute-start.4) | collective-permute-done | bytes 69664 | tf_op jit(solution)/shard_map/ppermute | solution.py:21
  185.7 1.6 fusion.27
  187.3 15.6 %reduce-scatter.2.cloned.1.call-done = f32[8,16,256]{2,1,0:T(8,128)} async-done(((f32[8,16,1024]{2,1,0:T(8,128)}), f32[8,16,256]{2,1,0:T(8,128)}) %reduce-scatter.2.cloned.1.call-update) | async-done | bytes 131088 | tf_op jit(solution)/shard_map/reduce_scatter | solution.py:158
  (134 shorter events, 17.3 us)
Async XLA Ops:
  23.9 5.9 %copy-start.2 = (f32[2,8,16,1024]{3,2,1,0:T(8,128)S(1)}, f32[2,8,16,1024]{3,2,1,0:T(8,128)}, u32[]{:S(2)}) copy-start(f32[2,8,16,1024]{3,2,1,0:T(8,128)} %param.11) | copy-start | bytes 3145732
  23.9 24.2 %all-to-all-start = ((f32[4,1,98304]{2,1,0:T(1,128)}), f32[4,1,98304]{2,1,0:T(1,128)S(1)}, u32[]{:S(2)}, u32[]{:S(2)}) async-start(f32[4,1,98304]{2,1,0:T(1,128)} %reshape.176), calls=%async_computation | async-start | bytes 3145728 | tf_op jit(solution)/shard_map/all_to_all | solution.py:147
  29.8 1.1 copy-start.10
  29.8 1.1 copy-start.12
  29.8 2.2 %copy-start.11 = (s32[16,256]{1,0:T(8,128)S(1)}, s32[16,256]{1,0:T(8,128)}, u32[]{:S(2)}) copy-start(s32[16,256]{1,0:T(8,128)} %param.19) | copy-start | bytes 49156
  48.1 1.2 copy-start.1
  75.9 17.5 %all-to-all-start.1 = ((f32[2,32,16,256]{3,2,0,1:T(8,128)}), f32[2,32,16,256]{3,2,0,1:T(8,128)}, u32[]{:S(2)}, u32[]{:S(2)}) async-start(f32[2,32,16,256]{3,2,0,1:T(8,128)} %copy.59), calls=%async_computation.1 | async-start | bytes 2097152 | tf_op jit(solution)/shard_map/all_to_all | solution.py:149
  85.2 20.7 %copy-start.8 = (f32[16,1024]{1,0:T(8,128)S(1)}, f32[16,1024]{1,0:T(8,128)}, u32[]{:S(2)}) copy-start(f32[16,1024]{1,0:T(8,128)} %param.16) | copy-start | bytes 196612
  85.2 20.8 %copy-start.9 = (f32[16,1024]{1,0:T(8,128)S(1)}, f32[16,1024]{1,0:T(8,128)}, u32[]{:S(2)}) copy-start(f32[16,1024]{1,0:T(8,128)} %param.14) | copy-start | bytes 196612
  93.4 58.9 %all-to-all-start.2 = ((f32[16,256,128]{2,0,1:T(8,128)}), f32[16,256,128]{2,0,1:T(8,128)}, u32[]{:S(2)}, u32[]{:S(2)}) async-start(f32[16,256,128]{2,0,1:T(8,128)} %multiply_bitcast_fusion), calls=%async_computation.2 | async-start | bytes 4194304 | tf_op jit(solution)/shard_map/all_to_all | solution.py:109
  103.0 99.9 %reduce-scatter.2.cloned.1.call-start = ((), (), s32[]{:S(2)}) async-start(), calls=%async_computation.4 | async-start | bytes 655360 | tf_op jit(solution)/shard_map/reduce_scatter | solution.py:158
  155.8 1.4 copy-start
  155.8 1.4 copy-start.7
  157.5 3.8 %collective-permute-start.1 = (f32[34,1,1024]{2,1,0:T(1,128)S(1)}, f32[34,1,1024]{2,1,0:T(1,128)S(1)}, u32[]{:S(2)}, u32[]{:S(2)}) collective-permute-start(f32[34,1,1024]{2,1,0:T(1,128)S(1)} %get-tuple-element.84), channel_id=1, source_target_pairs={{0,16},{16,32},{32,48},{48,64},{64,80},{80,96},{96,112},{112,128},... | collective-permute-start | bytes 417800 | tf_op jit(solution)/shard_map/ppermute | solution.py:19
  159.6 3.3 %collective-permute-start = (f32[34,1,1024]{2,1,0:T(1,128)S(1)}, f32[34,1,1024]{2,1,0:T(1,128)S(1)}, u32[]{:S(2)}, u32[]{:S(2)}) collective-permute-start(f32[34,1,1024]{2,1,0:T(1,128)S(1)} %get-tuple-element.83), channel_id=1, source_target_pairs={{16,0},{32,16},{48,32},{64,48},{80,64},{96,80},{112,96},{128,112},... | collective-permute-start | bytes 417800 | tf_op jit(solution)/shard_map/ppermute | solution.py:21
  163.6 8.6 %copy-start.6 = (f32[16,16,1023]{2,1,0:T(8,128)S(1)}, f32[16,16,1023]{2,1,0:T(8,128)}, u32[]{:S(2)}) copy-start(f32[16,16,1023]{2,1,0:T(8,128)} %get-tuple-element.96) | copy-start | bytes 3142660
  165.3 6.9 %copy-start.5 = (f32[16,16,1023]{2,1,0:T(8,128)S(1)}, f32[16,16,1023]{2,1,0:T(8,128)}, u32[]{:S(2)}) copy-start(f32[16,16,1023]{2,1,0:T(8,128)} %get-tuple-element.95) | copy-start | bytes 3142660
  165.4 10.7 %collective-permute-start.3 = (f32[17,1,1024]{2,1,0:T(1,128)S(1)}, f32[17,1,1024]{2,1,0:T(1,128)S(1)}, u32[]{:S(2)}, u32[]{:S(2)}) collective-permute-start(f32[17,1,1024]{2,1,0:T(1,128)S(1)} %get-tuple-element.88), channel_id=1, source_target_pairs={{0,16},{16,32},{32,48},{48,64},{64,80},{80,96},{96,112},{112,128},... | collective-permute-start | bytes 208904 | tf_op jit(solution)/shard_map/ppermute | solution.py:19
  170.7 5.7 %collective-permute-start.2 = (f32[17,1,1024]{2,1,0:T(1,128)S(1)}, f32[17,1,1024]{2,1,0:T(1,128)S(1)}, u32[]{:S(2)}, u32[]{:S(2)}) collective-permute-start(f32[17,1,1024]{2,1,0:T(1,128)S(1)} %get-tuple-element.87), channel_id=1, source_target_pairs={{16,0},{32,16},{48,32},{64,48},{80,64},{96,80},{112,96},{128,112},... | collective-permute-start | bytes 208904 | tf_op jit(solution)/shard_map/ppermute | solution.py:21
  176.1 1.2 copy-start.3
  176.1 1.5 copy-start.4
  178.4 4.7 %collective-permute-start.5 = (f32[17,1,1024]{2,1,0:T(1,128)S(1)}, f32[17,1,1024]{2,1,0:T(1,128)S(1)}, u32[]{:S(2)}, u32[]{:S(2)}) collective-permute-start(f32[17,1,1024]{2,1,0:T(1,128)S(1)} %get-tuple-element.86), channel_id=1, source_target_pairs={{0,16},{16,32},{32,48},{48,64},{64,80},{80,96},{96,112},{112,128},... | collective-permute-start | bytes 208904 | tf_op jit(solution)/shard_map/ppermute | solution.py:19
  181.8 3.9 %collective-permute-start.4 = (f32[17,1,1024]{2,1,0:T(1,128)S(1)}, f32[17,1,1024]{2,1,0:T(1,128)S(1)}, u32[]{:S(2)}, u32[]{:S(2)}) collective-permute-start(f32[17,1,1024]{2,1,0:T(1,128)S(1)} %get-tuple-element.85), channel_id=1, source_target_pairs={{16,0},{32,16},{48,32},{64,48},{80,64},{96,80},{112,96},{128,112},... | collective-permute-start | bytes 208904 | tf_op jit(solution)/shard_map/ppermute | solution.py:21
Sparse Core Ops, SparseCore 0:
  176.2 26.7 reduce-scatter.1
where the time goes:
time: 211 us; the launch traced here: 210 us
  waiting for transfers between devices  81.3 us (39%)
  local copies, waits for them, and re-layouts  49.5 us (23%)
  starting transfers between devices  35.7 us (17%)
  other arithmetic  24.7 us (12%)
  between operations  14.8 us (7%)
  matrix products  3.79 us (2%)
    all_to_all x1, waiting for transfers between devices, deliver(): lax.all_to_all(packed, 'tile', split_axis=1, concat_axis=1, tiled=True)  40.2 us
    unnamed x43, local copies, waits for them, and re-layouts  19.7 us
    reduce_scatter x1, waiting for transfers between devices, shards(): lax.psum_scatter(jnp.sum(parent_adjoint, axis=0), 'tag', scatter_dimensio...  15.6 us
    all_to_all x1, waiting for transfers between devices, shards(): lax.all_to_all(stacked, 'lev', split_axis=3, concat_axis=1, tiled=True)  13.4 us
    ppermute x3, starting transfers between devices, extended(): lax.ppermute(tail, axis, [(i, (i + 1) % count) for i in range(ends)])  10.3 us
    all_to_all x1, starting transfers between devices, deliver(): lax.all_to_all(packed, 'tile', split_axis=1, concat_axis=1, tiled=True)  9.61 us
    all_to_all x2, local copies, waits for them, and re-layouts, shards(): lax.all_to_all(stacked, 'lev', split_axis=3, concat_axis=1, tiled=True)  8.35 us
    all_to_all x1, waiting for transfers between devices, shards(): lax.all_to_all(column_result, 'lev', split_axis=1, concat_axis=3, tiled=T...  8.27 us
  transfers between devices with their start and end apart: 10, of which 6 were waited for; matrix products, arithmetic and copies ran while one was open for 12% of the time, Pallas kernels for 0%

commit v1 on v0

--- a/solution.py
+++ b/solution.py
@@ -6,6 +6,39 @@
 CAP = 16
 NSUB = 3
 HIGHEST = lax.Precision.HIGHEST
+
+
+def measure_rails_here(packet, in_dim, work_x):
+    piece_now = packet.shape
+    return jnp.moveaxis(
+        packet.reshape(
+            *piece_now[:in_dim], work_x, piece_now[in_dim] // work_x, *piece_now[in_dim + 1 :]
+        ),
+        in_dim,
+        0,
+    )
+
+
+def samples_all_handle(frame_in, join_dim):
+    later = list(frame_in.shape[1:])
+    later[join_dim] *= frame_in.shape[0]
+    return jnp.moveaxis(frame_in, 0, join_dim).reshape(later)
+
+
+def edit_the_levels_all(incoming_x, lane_axis, m, field_in):
+    f_now = lax.axis_size(lane_axis)
+    arr_now = lax.axis_index(lane_axis)
+    current_value, y1 = (f_now, arr_now)
+    current_block = measure_rails_here(incoming_x, m, current_value)
+    n_now = current_block
+    for k in range(1, current_value):
+        high, seen_now = ((y1 + k) % current_value, (y1 - k) % current_value)
+        p_next = lax.dynamic_index_in_dim(current_block, high, 0)
+        kept_arr = lax.ppermute(
+            p_next, lane_axis, [(at, (at + k) % current_value) for at in range(current_value)]
+        )
+        n_now = lax.dynamic_update_slice_in_dim(n_now, kept_arr, seen_now, axis=0)
+    return samples_all_handle(n_now, field_in)
 
 
 def extended(cells, sides, width):
@@ -146,7 +179,7 @@
     stacked = jnp.concatenate([parent_field, parent_mixing[None]], axis=0)
     columns = lax.all_to_all(stacked, "lev", split_axis=3, concat_axis=1, tiled=True)
     column_result = tridiagonal(columns[:tag_count], columns[tag_count])
-    solved = lax.all_to_all(column_result, "lev", split_axis=1, concat_axis=3, tiled=True)
+    solved = edit_the_levels_all(column_result, "lev", 1, 3)
     parent_adjoint, nest_adjoint = advance(
         nest_field + forcing,
         solved,

time: 211 us -> 174 us (0.82)
  waiting for transfers between devices: 81.3 us -> 38.9 us
  local copies, waits for them, and re-layouts: 49.5 us -> 54.1 us
    all_to_all x1, waiting for transfers between devices: 40.2 us -> 0.01 us  [deliver(): lax.all_to_all(packed, 'tile', split_axis=1, concat_axis=1, tiled=True)]
    ppermute x0 -> x3, waiting for transfers between devices: none -> 8.38 us  [edit_the_levels_all(): lax.ppermute(p_next, lane_axis, [(at, (at + k) % current_value) for at in...]
    all_to_all x1 -> x0, waiting for transfers between devices: 8.27 us -> none  [shards(): lax.all_to_all(column_result, 'lev', split_axis=1, concat_axis=3, tiled=T...]
    all_to_all x1 -> x0, starting transfers between devices: 5.69 us -> none  [shards(): lax.all_to_all(column_result, 'lev', split_axis=1, concat_axis=3, tiled=T...]
    all_to_all x1, waiting for transfers between devices: 13.4 us -> 7.95 us  [shards(): lax.all_to_all(stacked, 'lev', split_axis=3, concat_axis=1, tiled=True)]
    ppermute x0 -> x3, starting transfers between devices: none -> 4.17 us  [edit_the_levels_all(): lax.ppermute(p_next, lane_axis, [(at, (at + k) % current_value) for at in...]
    dynamic_update_slice x0 -> x3, local copies, waits for them, and re-layouts: none -> 2.9 us  [edit_the_levels_all(): n_now = lax.dynamic_update_slice_in_dim(n_now, kept_arr, seen_now, axis=0)]
    reduce_scatter x1, waiting for transfers between devices: 15.6 us -> 18.1 us  [shards(): lax.psum_scatter(jnp.sum(parent_adjoint, axis=0), 'tag', scatter_dimensio...]
  transfers between devices with their start and end apart: 10 -> 12, of which waited for: 6 -> 7; matrix products, arithmetic and copies ran while one was open for 12% -> 34% of each run, Pallas kernels for 0% -> 0%
where the time goes in v1:
time: 174 us; the launch traced here: 173 us
  local copies, waits for them, and re-layouts  54.1 us (31%)
  waiting for transfers between devices  38.9 us (22%)
  starting transfers between devices  34.8 us (20%)
  other arithmetic  26 us (15%)
  between operations  14.7 us (8%)
  matrix products  4.75 us (3%)
    unnamed x43, local copies, waits for them, and re-layouts  19.8 us
    reduce_scatter x1, waiting for transfers between devices, shards(): lax.psum_scatter(jnp.sum(parent_adjoint, axis=0), 'tag', scatter_dimensio...  18.1 us
    ppermute x3, starting transfers between devices, extended(): lax.ppermute(tail, axis, [(i, (i + 1) % count) for i in range(ends)])  11.1 us
    all_to_all x2, local copies, waits for them, and re-layouts, shards(): lax.all_to_all(stacked, 'lev', split_axis=3, concat_axis=1, tiled=True)  9.06 us
    all_to_all x1, starting transfers between devices, deliver(): lax.all_to_all(packed, 'tile', split_axis=1, concat_axis=1, tiled=True)  8.76 us
    ppermute x3, waiting for transfers between devices, edit_the_levels_all(): lax.ppermute(p_next, lane_axis, [(at, (at + k) % current_value) for at in...  8.38 us
    all_to_all x1, waiting for transfers between devices, shards(): lax.all_to_all(stacked, 'lev', split_axis=3, concat_axis=1, tiled=True)  7.95 us
    all_to_all x1, other arithmetic, shards(): lax.all_to_all(stacked, 'lev', split_axis=3, concat_axis=1, tiled=True)  7.31 us
  transfers between devices with their start and end apart: 12, of which 7 were waited for; matrix products, arithmetic and copies ran while one was open for 34% of the time, Pallas kernels for 0%

profile of v1, /device:TPU:2, one launch (start us, length us, event | category | flops | bytes accessed | tf_op | source)
XLA Modules:
  0.0 173.4 jit_solution(16299069669201103449)
XLA Ops:
  7.2 1.5 pad_maximum_fusion.5
  8.7 7.0 %copy.51 = f32[3,8,16,1024]{2,1,0,3:T(8,128)} copy(f32[3,8,16,1024]{3,2,1,0:T(8,128)S(1)} %pad_maximum_fusion.5) | data formatting | bytes 3145728 | tf_op jit(solution)/shard_map/concatenate | solution.py:179
  15.6 8.3 %reshape.178 = f32[4,1,98304]{2,1,0:T(1,128)} reshape(f32[1024,3,8,16]{3,2,1,0:T(8,128)} %bitcast.237) | data formatting | bytes 3145728
  23.9 6.7 %all-to-all-start = ((f32[4,1,98304]{2,1,0:T(1,128)}), f32[4,1,98304]{2,1,0:T(1,128)}, u32[]{:S(2)}, u32[]{:S(2)}) async-start(f32[4,1,98304]{2,1,0:T(1,128)} %reshape.178), calls=%async_computation | async-start | bytes 3145728 | tf_op jit(solution)/shard_map/all_to_all | solution.py:180
  37.9 2.5 %multiply_bitcast_fusion = f32[16,256,128]{2,0,1:T(8,128)} fusion(f32[256,16,128]{2,1,0:T(8,128)S(1)} %gather_fusion, f32[256]{0:T(256)S(1)} %convert_element_type.43, pred[256]{0:T(512)(128)(4,1)S(1)} %compare_and_fusion), kind=kLoop, calls=%fused_computation.5 | loop fusion | flops 1048576 | bytes 4195584 | tf_op jit(solution)/shard_map/mul | solution.py:141
  40.4 7.9 %all-to-all-done = f32[4,1,98304]{2,1,0:T(1,128)} async-done(((f32[4,1,98304]{2,1,0:T(1,128)}), f32[4,1,98304]{2,1,0:T(1,128)}, u32[]{:S(2)}, u32[]{:S(2)}) %all-to-all-start) | async-done | bytes 1572896 | tf_op jit(solution)/shard_map/all_to_all | solution.py:180
  48.3 8.8 %all-to-all-start.1 = ((f32[16,256,128]{2,0,1:T(8,128)}), f32[16,256,128]{2,0,1:T(8,128)S(1)}, u32[]{:S(2)}, u32[]{:S(2)}) async-start(f32[16,256,128]{2,0,1:T(8,128)} %multiply_bitcast_fusion), calls=%async_computation.1 | async-start | bytes 4194304 | tf_op jit(solution)/shard_map/all_to_all | solution.py:142
  57.9 7.3 %reduce.4 = f32[4,98304]{1,0:T(4,128)} reduce(f32[4,1,98304]{2,1,0:T(1,128)} %all-to-all-done, f32[]{:T(128)} %broadcast.2770), dimensions={1}, to_apply=%all_to_all.14.reduce_sub_computation | reduce | bytes 3145732 | tf_op jit(solution)/shard_map/all_to_all | solution.py:180
  65.2 10.5 %reshape.179 = f32[1024,3,8,16]{3,2,1,0:T(8,128)} reshape(f32[4,98304]{1,0:T(4,128)} %reduce.4) | data formatting | bytes 3145728
  75.7 8.6 %copy.63 = f32[3,8,16,4,256]{4,3,2,1,0:T(4,128)} copy(f32[3,8,16,4,256]{2,1,0,4,3:T(8,128)} %bitcast.238) | data formatting | bytes 3145728 | tf_op jit(solution)/shard_map/all_to_all | solution.py:180
  88.6 3.5 %collective-permute-start.1 = (f32[1,2,8,16,256]{4,3,2,0,1:T(8,128)}, f32[1,2,8,16,256]{4,3,2,0,1:T(8,128)}, u32[]{:S(2)}, u32[]{:S(2)}) collective-permute-start(f32[1,2,8,16,256]{4,3,2,0,1:T(8,128)} %get-tuple-element.98), channel_id=1, source_target_pairs={{0,8},{4,12},{8,0},{12,4},{1,9},{5,13},{9,1},{13,5},{2,10},{6,14},... | collective-permute-start | bytes 786440 | tf_op jit(solution)/shard_map/ppermute | solution.py:37
  94.6 3.4 %collective-permute-done = f32[1,2,8,16,256]{4,3,2,0,1:T(8,128)} collective-permute-done((f32[1,2,8,16,256]{4,3,2,0,1:T(8,128)}, f32[1,2,8,16,256]{4,3,2,0,1:T(8,128)}, u32[]{:S(2)}, u32[]{:S(2)}) %collective-permute-start) | collective-permute-done | bytes 262176 | tf_op jit(solution)/shard_map/ppermute | solution.py:37
  100.8 4.1 %collective-permute-done.2 = f32[1,2,8,16,256]{4,3,2,0,1:T(8,128)} collective-permute-done((f32[1,2,8,16,256]{4,3,2,0,1:T(8,128)}, f32[1,2,8,16,256]{4,3,2,0,1:T(8,128)}, u32[]{:S(2)}, u32[]{:S(2)}) %collective-permute-start.2) | collective-permute-done | bytes 262176 | tf_op jit(solution)/shard_map/ppermute | solution.py:37
  105.9 1.7 copy.55
  107.6 1.8 %reshape_reshape.3 = f32[16,16,1024]{2,1,0:T(8,128)S(1)} reshape(f32[2,8,16,4,256]{4,3,2,1,0:T(4,128)} %copy.55) | data formatting | bytes 2097152 | tf_op jit(solution)/shard_map/reshape;reshape | solution.py:110
  109.4 1.7 fusion.137
  111.1 3.7 %fusion.4 = f32[16,128,128]{2,1,0:T(8,128)} fusion(f32[256,128,1]{0,1,2:T(8,128)} %convolution_bitcast_fusion, f32[16,256,128]{2,0,1:T(8,128)S(1)} %all-to-all-done.1), kind=kOutput, calls=%fused_computation.12 | convolution fusion | flops 805306368 | bytes 3276800 | tf_op jit(solution)/shard_map/lic,ib->lbc/dot_general | solution.py:160
  114.8 1.5 reshape.163
  117.4 1.9 %collective-permute-start.4 = (f32[34,1,1024]{2,1,0:T(1,128)S(1)}, f32[34,1,1024]{2,1,0:T(1,128)S(1)}, u32[]{:S(2)}, u32[]{:S(2)}) collective-permute-start(f32[34,1,1024]{2,1,0:T(1,128)S(1)} %get-tuple-element.84), channel_id=1, source_target_pairs={{0,16},{16,32},{32,48},{48,64},{64,80},{80,96},{96,112},{112,128},... | collective-permute-start | bytes 417800 | tf_op jit(solution)/shard_map/ppermute | solution.py:52
  119.3 1.3 collective-permute-start.3
  121.1 2.8 %collective-permute-done.3 = f32[34,1,1024]{2,1,0:T(1,128)S(1)} collective-permute-done((f32[34,1,1024]{2,1,0:T(1,128)S(1)}, f32[34,1,1024]{2,1,0:T(1,128)S(1)}, u32[]{:S(2)}, u32[]{:S(2)}) %collective-permute-start.3) | collective-permute-done | bytes 139296 | tf_op jit(solution)/shard_map/ppermute | solution.py:54
  124.6 1.3 fusion.135
  126.7 6.1 %collective-permute-start.6 = (f32[17,1,1024]{2,1,0:T(1,128)}, f32[17,1,1024]{2,1,0:T(1,128)}, u32[]{:S(2)}, u32[]{:S(2)}) collective-permute-start(f32[17,1,1024]{2,1,0:T(1,128)} %get-tuple-element.88), channel_id=1, source_target_pairs={{0,16},{16,32},{32,48},{48,64},{64,80},{80,96},{96,112},{112,128},... | collective-permute-start | bytes 208904 | tf_op jit(solution)/shard_map/ppermute | solution.py:52
  132.8 1.3 collective-permute-start.5
  134.1 1.7 fusion.35
  135.8 2.2 %reduce_sum.39 = f32[8,16,1024]{2,1,0:T(8,128)} reduce(f32[2,8,16,1024]{3,2,1,0:T(8,128)} %bitcast.272, f32[]{:T(128)} %constant.95.clone.1), dimensions={0}, to_apply=%region_7.8 | reduce | flops 131072 | bytes 1572868 | tf_op jit(solution)/shard_map/reduce_sum | solution.py:192
  138.0 1.2 fusion.2
  140.0 3.0 %collective-permute-start.8 = (f32[17,1,1024]{2,1,0:T(1,128)S(1)}, f32[17,1,1024]{2,1,0:T(1,128)S(1)}, u32[]{:S(2)}, u32[]{:S(2)}) collective-permute-start(f32[17,1,1024]{2,1,0:T(1,128)S(1)} %get-tuple-element.86), channel_id=1, source_target_pairs={{0,16},{16,32},{32,48},{48,64},{64,80},{80,96},{96,112},{112,128},... | collective-permute-start | bytes 208904 | tf_op jit(solution)/shard_map/ppermute | solution.py:52
  143.5 1.3 collective-permute-start.7
  145.1 1.7 collective-permute-done.7
  146.8 1.6 fusion.27
  148.4 18.1 %reduce-scatter.2.cloned.1.call-done = f32[8,16,256]{2,1,0:T(8,128)} async-done(((f32[8,16,1024]{2,1,0:T(8,128)}), f32[8,16,256]{2,1,0:T(8,128)}) %reduce-scatter.2.cloned.1.call-update) | async-done | bytes 131088 | tf_op jit(solution)/shard_map/reduce_scatter | solution.py:191
  (141 shorter events, 22.7 us)
Async XLA Ops:
  23.9 6.7 %copy-start.10 = (s32[16,256]{1,0:T(8,128)S(1)}, s32[16,256]{1,0:T(8,128)}, u32[]{:S(2)}) copy-start(s32[16,256]{1,0:T(8,128)} %param.18) | copy-start | bytes 49156
  23.9 6.7 %copy-start.12 = (s32[16]{0:T(128)S(1)}, s32[16]{0:T(128)}, u32[]{:S(2)}) copy-start(s32[16]{0:T(128)} %param.21) | copy-start | bytes 196
  23.9 6.9 %copy-start.2 = (f32[2,8,16,1024]{3,2,1,0:T(8,128)S(1)}, f32[2,8,16,1024]{3,2,1,0:T(8,128)}, u32[]{:S(2)}) copy-start(f32[2,8,16,1024]{3,2,1,0:T(8,128)} %param.11) | copy-start | bytes 3145732
  23.9 24.4 %all-to-all-start = ((f32[4,1,98304]{2,1,0:T(1,128)}), f32[4,1,98304]{2,1,0:T(1,128)}, u32[]{:S(2)}, u32[]{:S(2)}) async-start(f32[4,1,98304]{2,1,0:T(1,128)} %reshape.178), calls=%async_computation | async-start | bytes 3145728 | tf_op jit(solution)/shard_map/all_to_all | solution.py:180
  30.6 1.2 copy-start.11
  48.3 62.7 %all-to-all-start.1 = ((f32[16,256,128]{2,0,1:T(8,128)}), f32[16,256,128]{2,0,1:T(8,128)S(1)}, u32[]{:S(2)}, u32[]{:S(2)}) async-start(f32[16,256,128]{2,0,1:T(8,128)} %multiply_bitcast_fusion), calls=%async_computation.1 | async-start | bytes 4194304 | tf_op jit(solution)/shard_map/all_to_all | solution.py:142
  57.1 109.4 %reduce-scatter.2.cloned.1.call-start = ((), (), s32[]{:S(2)}) async-start(), calls=%async_computation.3 | async-start | bytes 655360 | tf_op jit(solution)/shard_map/reduce_scatter | solution.py:191
  84.2 1.6 copy-start.1
  87.5 7.0 %copy-start.7 = (f32[16,1024]{1,0:T(8,128)S(1)}, f32[16,1024]{1,0:T(8,128)}, u32[]{:S(2)}) copy-start(f32[16,1024]{1,0:T(8,128)} %param.16) | copy-start | bytes 196612
  87.5 7.0 %copy-start.9 = (f32[16,1024]{1,0:T(8,128)S(1)}, f32[16,1024]{1,0:T(8,128)}, u32[]{:S(2)}) copy-start(f32[16,1024]{1,0:T(8,128)} %param.14) | copy-start | bytes 196612
  88.6 9.4 %collective-permute-start = (f32[1,2,8,16,256]{4,3,2,0,1:T(8,128)}, f32[1,2,8,16,256]{4,3,2,0,1:T(8,128)}, u32[]{:S(2)}, u32[]{:S(2)}) collective-permute-start(f32[1,2,8,16,256]{4,3,2,0,1:T(8,128)} %get-tuple-element.99), channel_id=1, source_target_pairs={{0,4},{4,8},{8,12},{12,0},{1,5},{5,9},{9,13},{13,1},{2,6},{6,10},{... | collective-permute-start | bytes 786440 | tf_op jit(solution)/shard_map/ppermute | solution.py:37
  88.6 11.2 %collective-permute-start.1 = (f32[1,2,8,16,256]{4,3,2,0,1:T(8,128)}, f32[1,2,8,16,256]{4,3,2,0,1:T(8,128)}, u32[]{:S(2)}, u32[]{:S(2)}) collective-permute-start(f32[1,2,8,16,256]{4,3,2,0,1:T(8,128)} %get-tuple-element.98), channel_id=1, source_target_pairs={{0,8},{4,12},{8,0},{12,4},{1,9},{5,13},{9,1},{13,5},{2,10},{6,14},... | collective-permute-start | bytes 786440 | tf_op jit(solution)/shard_map/ppermute | solution.py:37
  92.8 12.2 %collective-permute-start.2 = (f32[1,2,8,16,256]{4,3,2,0,1:T(8,128)}, f32[1,2,8,16,256]{4,3,2,0,1:T(8,128)}, u32[]{:S(2)}, u32[]{:S(2)}) collective-permute-start(f32[1,2,8,16,256]{4,3,2,0,1:T(8,128)} %get-tuple-element.97), channel_id=1, source_target_pairs={{0,12},{4,0},{8,4},{12,8},{1,13},{5,1},{9,5},{13,9},{2,14},{6,2},{... | collective-permute-start | bytes 786440 | tf_op jit(solution)/shard_map/ppermute | solution.py:37
  114.8 1.5 copy-start.8
  116.3 0.8 copy-start
  116.3 0.9 copy-start.6
  117.4 3.6 %collective-permute-start.4 = (f32[34,1,1024]{2,1,0:T(1,128)S(1)}, f32[34,1,1024]{2,1,0:T(1,128)S(1)}, u32[]{:S(2)}, u32[]{:S(2)}) collective-permute-start(f32[34,1,1024]{2,1,0:T(1,128)S(1)} %get-tuple-element.84), channel_id=1, source_target_pairs={{0,16},{16,32},{32,48},{48,64},{64,80},{80,96},{96,112},{112,128},... | collective-permute-start | bytes 417800 | tf_op jit(solution)/shard_map/ppermute | solution.py:52
  119.3 4.5 %collective-permute-start.3 = (f32[34,1,1024]{2,1,0:T(1,128)S(1)}, f32[34,1,1024]{2,1,0:T(1,128)S(1)}, u32[]{:S(2)}, u32[]{:S(2)}) collective-permute-start(f32[34,1,1024]{2,1,0:T(1,128)S(1)} %get-tuple-element.83), channel_id=1, source_target_pairs={{16,0},{32,16},{48,32},{64,48},{80,64},{96,80},{112,96},{128,112},... | collective-permute-start | bytes 417800 | tf_op jit(solution)/shard_map/ppermute | solution.py:54
  124.6 9.5 %copy-start.5 = (f32[16,16,1023]{2,1,0:T(8,128)S(1)}, f32[16,16,1023]{2,1,0:T(8,128)}, u32[]{:S(2)}) copy-start(f32[16,16,1023]{2,1,0:T(8,128)} %get-tuple-element.96) | copy-start | bytes 3142660
  125.9 8.2 %copy-start.4 = (f32[16,16,1023]{2,1,0:T(8,128)S(1)}, f32[16,16,1023]{2,1,0:T(8,128)}, u32[]{:S(2)}) copy-start(f32[16,16,1023]{2,1,0:T(8,128)} %get-tuple-element.95) | copy-start | bytes 3142660
  126.7 11.4 %collective-permute-start.6 = (f32[17,1,1024]{2,1,0:T(1,128)}, f32[17,1,1024]{2,1,0:T(1,128)}, u32[]{:S(2)}, u32[]{:S(2)}) collective-permute-start(f32[17,1,1024]{2,1,0:T(1,128)} %get-tuple-element.88), channel_id=1, source_target_pairs={{0,16},{16,32},{32,48},{48,64},{64,80},{80,96},{96,112},{112,128},... | collective-permute-start | bytes 208904 | tf_op jit(solution)/shard_map/ppermute | solution.py:52
  132.8 6.5 %collective-permute-start.5 = (f32[17,1,1024]{2,1,0:T(1,128)}, f32[17,1,1024]{2,1,0:T(1,128)S(1)}, u32[]{:S(2)}, u32[]{:S(2)}) collective-permute-start(f32[17,1,1024]{2,1,0:T(1,128)} %get-tuple-element.87), channel_id=1, source_target_pairs={{16,0},{32,16},{48,32},{64,48},{80,64},{96,80},{112,96},{128,112},... | collective-permute-start | bytes 208904 | tf_op jit(solution)/shard_map/ppermute | solution.py:54
  138.0 1.3 copy-start.3
  140.0 4.7 %collective-permute-start.8 = (f32[17,1,1024]{2,1,0:T(1,128)S(1)}, f32[17,1,1024]{2,1,0:T(1,128)S(1)}, u32[]{:S(2)}, u32[]{:S(2)}) collective-permute-start(f32[17,1,1024]{2,1,0:T(1,128)S(1)} %get-tuple-element.86), channel_id=1, source_target_pairs={{0,16},{16,32},{32,48},{48,64},{64,80},{80,96},{96,112},{112,128},... | collective-permute-start | bytes 208904 | tf_op jit(solution)/shard_map/ppermute | solution.py:52
  143.5 3.3 %collective-permute-start.7 = (f32[17,1,1024]{2,1,0:T(1,128)S(1)}, f32[17,1,1024]{2,1,0:T(1,128)S(1)}, u32[]{:S(2)}, u32[]{:S(2)}) collective-permute-start(f32[17,1,1024]{2,1,0:T(1,128)S(1)} %get-tuple-element.85), channel_id=1, source_target_pairs={{16,0},{32,16},{48,32},{64,48},{80,64},{96,80},{112,96},{128,112},... | collective-permute-start | bytes 208904 | tf_op jit(solution)/shard_map/ppermute | solution.py:54
Sparse Core Ops, SparseCore 0:
  138.1 28.3 reduce-scatter.1
